TPU v7x, 512 devices: a whole 4x8x8 slice. The times are simulated.
512 devices in a mesh: tm: 64 (over z, y), space: 8 (over x, core).
Axes of the slice: x: 4, y: 8, z: 8, core: 2. Of those that a mesh axis runs over, the one named last changes fastest.
Arguments:
- frames: bfloat16 [128, 32, 64, 256], P('tm', 'space'), may hold values from -54 to 54
- cotangent: bfloat16 [128, 32, 64, 256], P('tm', 'space'), may hold values from -6 to 6
- w_spatial: bfloat16 [3, 3, 256, 256], replicated, may hold values from -0.125 to 0.125
- w_temporal: bfloat16 [3, 256, 256], replicated, may hold values from -0.21875 to 0.21875
- norm_gain: float32 [256], replicated, may hold values from 0.1 to 1.9
- w_query: bfloat16 [256, 256], replicated, may hold values from -0.375 to 0.375
- w_key: bfloat16 [256, 256], replicated, may hold values from -0.375 to 0.375
- w_value: bfloat16 [256, 256], replicated, may hold values from -0.375 to 0.375
- w_out: bfloat16 [256, 256], replicated, may hold values from -0.375 to 0.375
Outputs:
- input_grad: bfloat16 [128, 32, 64, 256], P('tm', 'space')
All inputs are finite; a program needn't handle non-finite values.
Results may differ from a plain program's by a relative error of at most 0.017.
Values may be sent and summed in bfloat16 or wider, within the bound.
A program may use at most 64 MiB of HBM per device.

v0:
```python
import math

import jax
import jax.numpy as jnp
from jax import lax
from jax.sharding import PartitionSpec as P

EPSILON = 1e-05


def with_halo(cells, sides, width):
    for axis, dim in sides:
        count = lax.axis_size(axis)
        ends = count - 1
        head = lax.slice_in_dim(cells, 0, width, axis=dim)
        tail = lax.slice_in_dim(cells, cells.shape[dim] - width, cells.shape[dim], axis=dim)
        cells = jnp.concatenate(
            [
                lax.ppermute(tail, axis, [(i, (i + 1) % count) for i in range(ends)]),
                cells,
                lax.ppermute(head, axis, [((i + 1) % count, i) for i in range(ends)]),
            ],
            axis=dim,
        )
    return cells


def shifted(block, axis, distance):
    devices = range(lax.axis_size(axis))
    route = [(i - distance, i) for i in devices if i - distance in devices]
    return lax.ppermute(block, axis, route)


def contract_last(left, weight):
    return lax.dot_general(
        left, weight, (((left.ndim - 1,), (1,)), ((), ())), preferred_element_type=jnp.float32
    )


def project(normed, weight):
    return jnp.dot(normed, weight, preferred_element_type=jnp.float32).astype(jnp.bfloat16)


def spatial_forward(frames, w_spatial):
    frame_count, row_count, col_count, channels = frames.shape
    rimmed = with_halo(frames, (("space", 1),), 1)
    padded = jnp.pad(rimmed, ((0, 0), (0, 0), (1, 1), (0, 0)))
    running = jnp.zeros((frame_count * row_count * col_count, channels), jnp.float32)
    for tap_row in range(3):
        for tap_col in range(3):
            window = padded[
                :, tap_row : tap_row + row_count, tap_col : tap_col + col_count
            ].reshape(-1, channels)
            running = running + jnp.dot(
                window, w_spatial[tap_row, tap_col], preferred_element_type=jnp.float32
            )
    return running.astype(jnp.bfloat16).reshape(frames.shape)


def temporal_forward(spatial, frames, w_temporal):
    channels = frames.shape[-1]
    previous = shifted(spatial, "tm", 1)
    extended = jnp.concatenate([previous, spatial], 0)
    stacked = jnp.concatenate([extended[2:], extended[1:-1], extended[:-2]], -1)
    mixed_sum = jnp.dot(
        stacked.reshape(-1, 3 * channels),
        w_temporal.reshape(3 * channels, channels),
        preferred_element_type=jnp.float32,
    )
    return (frames.astype(jnp.float32) + mixed_sum.reshape(frames.shape)).astype(jnp.bfloat16)


def norm_forward(hidden, norm_gain):
    hidden_wide = hidden.astype(jnp.float32)
    inverse = lax.rsqrt(jnp.mean(hidden_wide * hidden_wide, axis=-1, keepdims=True) + EPSILON)
    normed = (hidden_wide * inverse * norm_gain).astype(jnp.bfloat16)
    return (hidden_wide, inverse, normed)


def norm_backward(hidden_wide, inverse, norm_gain, normed_grad):
    scaled = normed_grad * norm_gain
    cubed = inverse * inverse * inverse
    result = inverse * scaled - hidden_wide * cubed * jnp.mean(
        hidden_wide * scaled, axis=-1, keepdims=True
    )
    return result.astype(jnp.bfloat16)


def attention_grads(query_rows, key_rows, value_rows, out_grad):
    frame_total = query_rows.shape[0]
    score_scale = 1.0 / math.sqrt(query_rows.shape[-1])
    query_index = lax.broadcasted_iota(jnp.int32, (frame_total, frame_total), 0)
    key_index = lax.broadcasted_iota(jnp.int32, (frame_total, frame_total), 1)
    causal_mask = key_index <= query_index
    scores = (
        jnp.einsum("fpc,gpc->pfg", query_rows, key_rows, preferred_element_type=jnp.float32)
        * score_scale
    )
    weights = jnp.where(causal_mask[None], jnp.exp(scores), 0.0)
    attn_probs = weights / jnp.sum(weights, axis=-1, keepdims=True)
    probs_low = attn_probs.astype(jnp.bfloat16)
    prob_grad = jnp.einsum("fpc,gpc->pfg", out_grad, value_rows, preferred_element_type=jnp.float32)
    value_grad = jnp.einsum(
        "pfg,fpc->gpc", probs_low, out_grad, preferred_element_type=jnp.float32
    ).astype(jnp.bfloat16)
    centre = jnp.sum(attn_probs * prob_grad, axis=-1, keepdims=True)
    score_grad = (attn_probs * (prob_grad - centre) * score_scale).astype(jnp.bfloat16)
    query_grad = jnp.einsum(
        "pfg,gpc->fpc", score_grad, key_rows, preferred_element_type=jnp.float32
    ).astype(jnp.bfloat16)
    key_grad = jnp.einsum(
        "pfg,fpc->gpc", score_grad, query_rows, preferred_element_type=jnp.float32
    ).astype(jnp.bfloat16)
    return (query_grad, key_grad, value_grad)


def to_groups(tensor, groups):
    return tensor.reshape(tensor.shape[0], groups, -1, tensor.shape[-1])


def body(frames, cotangent, w_spatial, w_temporal, norm_gain, w_query, w_key, w_value, w_out):
    groups = lax.axis_size("tm")
    frame_count, row_count, col_count, channels = frames.shape
    spatial = spatial_forward(frames, w_spatial)
    hidden = temporal_forward(spatial, frames, w_temporal)
    hidden_wide, inverse, normed = norm_forward(hidden, norm_gain)
    query_rows = project(normed, w_query)
    key_rows = project(normed, w_key)
    value_rows = project(normed, w_value)
    out_grad = contract_last(cotangent, w_out).astype(jnp.bfloat16)
    pieces = (
        lax.all_to_all(
            to_groups(query_rows, groups), "tm", split_axis=1, concat_axis=0, tiled=True
        ),
        lax.all_to_all(to_groups(key_rows, groups), "tm", split_axis=1, concat_axis=0, tiled=True),
        lax.all_to_all(
            to_groups(value_rows, groups), "tm", split_axis=1, concat_axis=0, tiled=True
        ),
        lax.all_to_all(to_groups(out_grad, groups), "tm", split_axis=1, concat_axis=0, tiled=True),
    )
    query_p, key_p, value_p, grad_p = [portion[:, 0] for portion in pieces]
    query_grad, key_grad, value_grad = attention_grads(query_p, key_p, value_p, grad_p)
    back_query = lax.all_to_all(query_grad[:, None], "tm", split_axis=0, concat_axis=1, tiled=True)
    back_key = lax.all_to_all(key_grad[:, None], "tm", split_axis=0, concat_axis=1, tiled=True)
    back_value = lax.all_to_all(value_grad[:, None], "tm", split_axis=0, concat_axis=1, tiled=True)
    normed_grad = contract_last(back_query.reshape(frames.shape), w_query)
    normed_grad = normed_grad + contract_last(back_key.reshape(frames.shape), w_key)
    normed_grad = normed_grad + contract_last(back_value.reshape(frames.shape), w_value)
    attn_grad = norm_backward(hidden_wide, inverse, norm_gain, normed_grad)
    total_grad = (cotangent.astype(jnp.float32) + attn_grad.astype(jnp.float32)).astype(
        jnp.bfloat16
    )
    upcoming = shifted(total_grad, "tm", -1)
    ahead_frames = jnp.concatenate([total_grad, upcoming], 0)
    flat_back = jnp.transpose(w_temporal, (0, 2, 1)).reshape(3 * channels, channels)
    stacked = jnp.concatenate([ahead_frames[:-2], ahead_frames[1:-1], ahead_frames[2:]], -1)
    spatial_grad = jnp.dot(
        stacked.reshape(-1, 3 * channels), flat_back, preferred_element_type=jnp.float32
    )
    spatial_grad = spatial_grad.astype(jnp.bfloat16).reshape(frames.shape)
    rimmed = with_halo(spatial_grad, (("space", 1),), 1)
    padded = jnp.pad(rimmed, ((0, 0), (0, 0), (1, 1), (0, 0)))
    running = total_grad.astype(jnp.float32).reshape(-1, channels)
    for tap_row in range(3):
        for tap_col in range(3):
            window = padded[
                :, 2 - tap_row : 2 - tap_row + row_count, 2 - tap_col : 2 - tap_col + col_count
            ].reshape(-1, channels)
            running = running + contract_last(window, w_spatial[tap_row, tap_col])
    return running.astype(jnp.bfloat16).reshape(frames.shape)


def solution(mesh):
    return jax.shard_map(
        body,
        mesh=mesh,
        in_specs=(
            P("tm", "space", None, None),
            P("tm", "space", None, None),
            P(),
            P(),
            P(),
            P(),
            P(),
            P(),
            P(),
        ),
        out_specs=P("tm", "space", None, None),
        check_vma=False,
    )
```

profile of v0, /device:TPU:1, one launch (start us, length us, event | category | flops | bytes accessed | tf_op | source)
XLA Modules:
  0.0 188.6 jit_solution(1084534786628643740)
XLA Ops:
  0.0 0.9 fusion.101
  0.9 4.5 %collective-permute-start = (bf16[2,1,64,256]{3,2,1,0:T(8,128)(2,1)S(1)}, bf16[2,1,64,256]{3,2,1,0:T(8,128)(2,1)S(1)}, u32[]{:S(2)}, u32[]{:S(2)}) collective-permute-start(bf16[2,1,64,256]{3,2,1,0:T(8,128)(2,1)S(1)} %get-tuple-element.23), channel_id=1, source_target_pairs={{0,1},{1,2},{2,3},{3,4},{4,5},{5,6},{6,7},{8,9},{9,10},{10,11},{11... | collective-permute-start | bytes 196616 | tf_op jit(solution)/shard_map/ppermute | solution.py:19
  5.4 5.6 %collective-permute-start.1 = (bf16[2,1,64,256]{3,2,1,0:T(8,128)(2,1)S(1)}, bf16[2,1,64,256]{3,2,1,0:T(8,128)(2,1)S(1)}, u32[]{:S(2)}, u32[]{:S(2)}) collective-permute-start(bf16[2,1,64,256]{3,2,1,0:T(8,128)(2,1)S(1)} %get-tuple-element.24), channel_id=1, source_target_pairs={{1,0},{2,1},{3,2},{4,3},{5,4},{6,5},{7,6},{9,8},{10,9},{11,10},{12... | collective-permute-start | bytes 196616 | tf_op jit(solution)/shard_map/ppermute | solution.py:21
  11.9 1.1 select_maximum_fusion.2
  13.2 1.0 copy-done.1
  16.4 2.5 %collective-permute-start.2 = (bf16[2,4,64,256]{3,2,1,0:T(8,128)(2,1)S(1)}, bf16[2,4,64,256]{3,2,1,0:T(8,128)(2,1)S(1)}, u32[]{:S(2)}, u32[]{:S(2)}) collective-permute-start(bf16[2,4,64,256]{3,2,1,0:T(8,128)(2,1)S(1)} %bitcast.221), channel_id=1, source_target_pairs={{0,8},{8,16},{16,24},{24,32},{32,40},{40,48},{48,56},{56,64},{64,7... | collective-permute-start | bytes 786440 | tf_op jit(solution)/shard_map/ppermute | solution.py:31
  20.1 15.4 %all-to-all-start.2 = ((bf16[2,64,4,256]{3,2,0,1:T(4,128)(2,1)}), bf16[2,64,4,256]{3,2,0,1:T(4,128)(2,1)S(1)}, u32[]{:S(2)}, u32[]{:S(2)}) async-start(bf16[2,64,4,256]{3,2,0,1:T(4,128)(2,1)} %copy.44), calls=%async_computation.2 | async-start | bytes 524288 | tf_op jit(solution)/shard_map/all_to_all | solution.py:139
  37.5 11.7 %all-to-all-done.2 = bf16[2,64,4,256]{3,2,0,1:T(4,128)(2,1)S(1)} async-done(((bf16[2,64,4,256]{3,2,0,1:T(4,128)(2,1)}), bf16[2,64,4,256]{3,2,0,1:T(4,128)(2,1)S(1)}, u32[]{:S(2)}, u32[]{:S(2)}) %all-to-all-start.2) | async-done | bytes 262176 | tf_op jit(solution)/shard_map/all_to_all | solution.py:139
  49.3 4.6 %all-to-all-start = ((bf16[2,64,4,256]{3,2,0,1:T(4,128)(2,1)}), bf16[2,64,4,256]{3,2,0,1:T(4,128)(2,1)S(1)}, u32[]{:S(2)}, u32[]{:S(2)}) async-start(bf16[2,64,4,256]{3,2,0,1:T(4,128)(2,1)} %copy.40), calls=%async_computation | async-start | bytes 524288 | tf_op jit(solution)/shard_map/all_to_all | solution.py:135
  55.0 13.3 %all-to-all-done = bf16[2,64,4,256]{3,2,0,1:T(4,128)(2,1)S(1)} async-done(((bf16[2,64,4,256]{3,2,0,1:T(4,128)(2,1)}), bf16[2,64,4,256]{3,2,0,1:T(4,128)(2,1)S(1)}, u32[]{:S(2)}, u32[]{:S(2)}) %all-to-all-start) | async-done | bytes 262176 | tf_op jit(solution)/shard_map/all_to_all | solution.py:135
  68.4 4.8 %all-to-all-start.3 = ((bf16[2,64,4,256]{3,2,0,1:T(4,128)(2,1)}), bf16[2,64,4,256]{3,2,0,1:T(4,128)(2,1)S(1)}, u32[]{:S(2)}, u32[]{:S(2)}) async-start(bf16[2,64,4,256]{3,2,0,1:T(4,128)(2,1)} %copy.46), calls=%async_computation.3 | async-start | bytes 524288 | tf_op jit(solution)/shard_map/all_to_all | solution.py:136
  74.2 11.8 %all-to-all-done.3 = bf16[2,64,4,256]{3,2,0,1:T(4,128)(2,1)S(1)} async-done(((bf16[2,64,4,256]{3,2,0,1:T(4,128)(2,1)}), bf16[2,64,4,256]{3,2,0,1:T(4,128)(2,1)S(1)}, u32[]{:S(2)}, u32[]{:S(2)}) %all-to-all-start.3) | async-done | bytes 262176 | tf_op jit(solution)/shard_map/all_to_all | solution.py:136
  86.0 5.6 %all-to-all-start.1 = ((bf16[2,64,4,256]{3,2,0,1:T(4,128)(2,1)}), bf16[2,64,4,256]{3,2,0,1:T(4,128)(2,1)S(1)}, u32[]{:S(2)}, u32[]{:S(2)}) async-start(bf16[2,64,4,256]{3,2,0,1:T(4,128)(2,1)} %copy.42), calls=%async_computation.1 | async-start | bytes 524288 | tf_op jit(solution)/shard_map/all_to_all | solution.py:132
  92.4 11.7 %all-to-all-done.1 = bf16[2,64,4,256]{3,2,0,1:T(4,128)(2,1)S(1)} async-done(((bf16[2,64,4,256]{3,2,0,1:T(4,128)(2,1)}), bf16[2,64,4,256]{3,2,0,1:T(4,128)(2,1)S(1)}, u32[]{:S(2)}, u32[]{:S(2)}) %all-to-all-start.1) | async-done | bytes 262176 | tf_op jit(solution)/shard_map/all_to_all | solution.py:132
  104.1 1.0 fusion.72
  105.1 1.0 fusion.10
  106.1 1.8 copy.54
  107.9 4.9 %all-to-all-start.5 = ((bf16[128,1,4,256]{3,2,1,0:T(4,128)(2,1)}), bf16[128,1,4,256]{3,2,1,0:T(4,128)(2,1)S(1)}, u32[]{:S(2)}, u32[]{:S(2)}) async-start(bf16[128,1,4,256]{3,2,1,0:T(4,128)(2,1)} %copy.54), calls=%async_computation.5 | async-start | bytes 524288 | tf_op jit(solution)/shard_map/all_to_all | solution.py:144
  112.8 1.0 fusion.9
  113.8 1.8 copy.50
  115.6 9.7 %all-to-all-done.5 = bf16[128,1,4,256]{3,2,1,0:T(4,128)(2,1)S(1)} async-done(((bf16[128,1,4,256]{3,2,1,0:T(4,128)(2,1)}), bf16[128,1,4,256]{3,2,1,0:T(4,128)(2,1)S(1)}, u32[]{:S(2)}, u32[]{:S(2)}) %all-to-all-start.5) | async-done | bytes 262176 | tf_op jit(solution)/shard_map/all_to_all | solution.py:144
  125.3 4.6 %all-to-all-start.4 = ((bf16[128,1,4,256]{3,2,1,0:T(4,128)(2,1)}), bf16[128,1,4,256]{3,2,1,0:T(4,128)(2,1)S(1)}, u32[]{:S(2)}, u32[]{:S(2)}) async-start(bf16[128,1,4,256]{3,2,1,0:T(4,128)(2,1)} %copy.50), calls=%async_computation.4 | async-start | bytes 524288 | tf_op jit(solution)/shard_map/all_to_all | solution.py:143
  131.0 11.4 %all-to-all-done.4 = bf16[128,1,4,256]{3,2,1,0:T(4,128)(2,1)S(1)} async-done(((bf16[128,1,4,256]{3,2,1,0:T(4,128)(2,1)}), bf16[128,1,4,256]{3,2,1,0:T(4,128)(2,1)S(1)}, u32[]{:S(2)}, u32[]{:S(2)}) %all-to-all-start.4) | async-done | bytes 262176 | tf_op jit(solution)/shard_map/all_to_all | solution.py:143
  142.4 4.8 %all-to-all-start.6 = ((bf16[128,1,4,256]{3,2,1,0:T(4,128)(2,1)}), bf16[128,1,4,256]{3,2,1,0:T(4,128)(2,1)S(1)}, u32[]{:S(2)}, u32[]{:S(2)}) async-start(bf16[128,1,4,256]{3,2,1,0:T(4,128)(2,1)} %copy.58), calls=%async_computation.6 | async-start | bytes 524288 | tf_op jit(solution)/shard_map/all_to_all | solution.py:145
  147.8 11.7 %all-to-all-done.6 = bf16[128,1,4,256]{3,2,1,0:T(4,128)(2,1)S(1)} async-done(((bf16[128,1,4,256]{3,2,1,0:T(4,128)(2,1)}), bf16[128,1,4,256]{3,2,1,0:T(4,128)(2,1)S(1)}, u32[]{:S(2)}, u32[]{:S(2)}) %all-to-all-start.6) | async-done | bytes 262176 | tf_op jit(solution)/shard_map/all_to_all | solution.py:145
  159.7 1.2 convolution_add_fusion.9
  161.6 1.3 collective-permute-start.3
  163.0 5.6 %collective-permute-done.3 = bf16[2,4,64,256]{3,2,1,0:T(8,128)(2,1)S(1)} collective-permute-done((bf16[2,4,64,256]{3,2,1,0:T(8,128)(2,1)S(1)}, bf16[2,4,64,256]{3,2,1,0:T(8,128)(2,1)S(1)}, u32[]{:S(2)}, u32[]{:S(2)}) %collective-permute-start.3) | collective-permute-done | bytes 262176 | tf_op jit(solution)/shard_map/ppermute | solution.py:31
  169.1 10.4 %collective-permute-start.4 = (bf16[2,1,64,256]{3,2,1,0:T(8,128)(2,1)S(1)}, bf16[2,1,64,256]{3,2,1,0:T(8,128)(2,1)S(1)}, u32[]{:S(2)}, u32[]{:S(2)}) collective-permute-start(bf16[2,1,64,256]{3,2,1,0:T(8,128)(2,1)S(1)} %get-tuple-element.19), channel_id=1, source_target_pairs={{0,1},{1,2},{2,3},{3,4},{4,5},{5,6},{6,7},{8,9},{9,10},{10,11},{11... | collective-permute-start | bytes 196616 | tf_op jit(solution)/shard_map/ppermute | solution.py:19
  179.5 1.9 %collective-permute-start.5 = (bf16[2,1,64,256]{3,2,1,0:T(8,128)(2,1)S(1)}, bf16[2,1,64,256]{3,2,1,0:T(8,128)(2,1)S(1)}, u32[]{:S(2)}, u32[]{:S(2)}) collective-permute-start(bf16[2,1,64,256]{3,2,1,0:T(8,128)(2,1)S(1)} %get-tuple-element.20), channel_id=1, source_target_pairs={{1,0},{2,1},{3,2},{4,3},{5,4},{6,5},{7,6},{9,8},{10,9},{11,10},{12... | collective-permute-start | bytes 196616 | tf_op jit(solution)/shard_map/ppermute | solution.py:21
  181.5 3.6 %collective-permute-done.5 = bf16[2,1,64,256]{3,2,1,0:T(8,128)(2,1)S(1)} collective-permute-done((bf16[2,1,64,256]{3,2,1,0:T(8,128)(2,1)S(1)}, bf16[2,1,64,256]{3,2,1,0:T(8,128)(2,1)S(1)}, u32[]{:S(2)}, u32[]{:S(2)}) %collective-permute-start.5) | collective-permute-done | bytes 65568 | tf_op jit(solution)/shard_map/ppermute | solution.py:21
  187.6 1.0 fusion.6
  (78 shorter events, 14.9 us)
Async XLA Ops:
  0.0 53.9 %copy-start = (bf16[256,256]{1,0:T(8,128)(2,1)S(1)}, bf16[256,256]{1,0:T(8,128)(2,1)}, u32[]{:S(2)}) copy-start(bf16[256,256]{1,0:T(8,128)(2,1)} %param.16) | copy-start | bytes 393220
  0.9 10.1 %collective-permute-start = (bf16[2,1,64,256]{3,2,1,0:T(8,128)(2,1)S(1)}, bf16[2,1,64,256]{3,2,1,0:T(8,128)(2,1)S(1)}, u32[]{:S(2)}, u32[]{:S(2)}) collective-permute-start(bf16[2,1,64,256]{3,2,1,0:T(8,128)(2,1)S(1)} %get-tuple-element.23), channel_id=1, source_target_pairs={{0,1},{1,2},{2,3},{3,4},{4,5},{5,6},{6,7},{8,9},{9,10},{10,11},{11... | collective-permute-start | bytes 196616 | tf_op jit(solution)/shard_map/ppermute | solution.py:19
  5.4 6.5 %collective-permute-start.1 = (bf16[2,1,64,256]{3,2,1,0:T(8,128)(2,1)S(1)}, bf16[2,1,64,256]{3,2,1,0:T(8,128)(2,1)S(1)}, u32[]{:S(2)}, u32[]{:S(2)}) collective-permute-start(bf16[2,1,64,256]{3,2,1,0:T(8,128)(2,1)S(1)} %get-tuple-element.24), channel_id=1, source_target_pairs={{1,0},{2,1},{3,2},{4,3},{5,4},{6,5},{7,6},{9,8},{10,9},{11,10},{12... | collective-permute-start | bytes 196616 | tf_op jit(solution)/shard_map/ppermute | solution.py:21
  13.0 1.3 copy-start.1
  13.2 1.5 copy-start.2
  16.2 2.8 %copy-start.3 = (bf16[2,4,64,256]{3,2,1,0:T(8,128)(2,1)S(1)}, bf16[2,4,64,256]{3,2,1,0:T(8,128)(2,1)}, u32[]{:S(2)}) copy-start(bf16[2,4,64,256]{3,2,1,0:T(8,128)(2,1)} %param.10) | copy-start | bytes 786436
  16.2 2.8 %copy-start.8 = (bf16[256,256]{1,0:T(8,128)(2,1)S(1)}, bf16[256,256]{1,0:T(8,128)(2,1)}, u32[]{:S(2)}) copy-start(bf16[256,256]{1,0:T(8,128)(2,1)} %param.17) | copy-start | bytes 393220
  16.4 19.1 %copy-start.6 = (bf16[3,256,256]{2,1,0:T(8,128)(2,1)S(1)}, bf16[3,256,256]{2,1,0:T(8,128)(2,1)}, u32[]{:S(2)}) copy-start(bf16[3,256,256]{2,1,0:T(8,128)(2,1)} %param.12) | copy-start | bytes 1179652
  16.4 19.1 %collective-permute-start.2 = (bf16[2,4,64,256]{3,2,1,0:T(8,128)(2,1)S(1)}, bf16[2,4,64,256]{3,2,1,0:T(8,128)(2,1)S(1)}, u32[]{:S(2)}, u32[]{:S(2)}) collective-permute-start(bf16[2,4,64,256]{3,2,1,0:T(8,128)(2,1)S(1)} %bitcast.221), channel_id=1, source_target_pairs={{0,8},{8,16},{16,24},{24,32},{32,40},{40,48},{48,56},{56,64},{64,7... | collective-permute-start | bytes 786440 | tf_op jit(solution)/shard_map/ppermute | solution.py:31
  20.1 29.2 %all-to-all-start.2 = ((bf16[2,64,4,256]{3,2,0,1:T(4,128)(2,1)}), bf16[2,64,4,256]{3,2,0,1:T(4,128)(2,1)S(1)}, u32[]{:S(2)}, u32[]{:S(2)}) async-start(bf16[2,64,4,256]{3,2,0,1:T(4,128)(2,1)} %copy.44), calls=%async_computation.2 | async-start | bytes 524288 | tf_op jit(solution)/shard_map/all_to_all | solution.py:139
  35.5 0.7 copy-start.9
  35.5 0.9 copy-start.5
  49.3 19.1 %all-to-all-start = ((bf16[2,64,4,256]{3,2,0,1:T(4,128)(2,1)}), bf16[2,64,4,256]{3,2,0,1:T(4,128)(2,1)S(1)}, u32[]{:S(2)}, u32[]{:S(2)}) async-start(bf16[2,64,4,256]{3,2,0,1:T(4,128)(2,1)} %copy.40), calls=%async_computation | async-start | bytes 524288 | tf_op jit(solution)/shard_map/all_to_all | solution.py:135
  53.9 19.2 %copy-start.4 = (bf16[256,256]{1,0:T(8,128)(2,1)S(1)}, bf16[256,256]{1,0:T(8,128)(2,1)}, u32[]{:S(2)}) copy-start(bf16[256,256]{1,0:T(8,128)(2,1)} %param.14) | copy-start | bytes 393220
  68.4 17.7 %all-to-all-start.3 = ((bf16[2,64,4,256]{3,2,0,1:T(4,128)(2,1)}), bf16[2,64,4,256]{3,2,0,1:T(4,128)(2,1)S(1)}, u32[]{:S(2)}, u32[]{:S(2)}) async-start(bf16[2,64,4,256]{3,2,0,1:T(4,128)(2,1)} %copy.46), calls=%async_computation.3 | async-start | bytes 524288 | tf_op jit(solution)/shard_map/all_to_all | solution.py:136
  86.0 18.1 %all-to-all-start.1 = ((bf16[2,64,4,256]{3,2,0,1:T(4,128)(2,1)}), bf16[2,64,4,256]{3,2,0,1:T(4,128)(2,1)S(1)}, u32[]{:S(2)}, u32[]{:S(2)}) async-start(bf16[2,64,4,256]{3,2,0,1:T(4,128)(2,1)} %copy.42), calls=%async_computation.1 | async-start | bytes 524288 | tf_op jit(solution)/shard_map/all_to_all | solution.py:132
  107.9 17.4 %all-to-all-start.5 = ((bf16[128,1,4,256]{3,2,1,0:T(4,128)(2,1)}), bf16[128,1,4,256]{3,2,1,0:T(4,128)(2,1)S(1)}, u32[]{:S(2)}, u32[]{:S(2)}) async-start(bf16[128,1,4,256]{3,2,1,0:T(4,128)(2,1)} %copy.54), calls=%async_computation.5 | async-start | bytes 524288 | tf_op jit(solution)/shard_map/all_to_all | solution.py:144
  125.3 17.2 %all-to-all-start.4 = ((bf16[128,1,4,256]{3,2,1,0:T(4,128)(2,1)}), bf16[128,1,4,256]{3,2,1,0:T(4,128)(2,1)S(1)}, u32[]{:S(2)}, u32[]{:S(2)}) async-start(bf16[128,1,4,256]{3,2,1,0:T(4,128)(2,1)} %copy.50), calls=%async_computation.4 | async-start | bytes 524288 | tf_op jit(solution)/shard_map/all_to_all | solution.py:143
  142.4 17.1 %all-to-all-start.6 = ((bf16[128,1,4,256]{3,2,1,0:T(4,128)(2,1)}), bf16[128,1,4,256]{3,2,1,0:T(4,128)(2,1)S(1)}, u32[]{:S(2)}, u32[]{:S(2)}) async-start(bf16[128,1,4,256]{3,2,1,0:T(4,128)(2,1)} %copy.58), calls=%async_computation.6 | async-start | bytes 524288 | tf_op jit(solution)/shard_map/all_to_all | solution.py:145
  161.3 1.6 copy-start.7
  161.6 7.1 %collective-permute-start.3 = (bf16[2,4,64,256]{3,2,1,0:T(8,128)(2,1)S(1)}, bf16[2,4,64,256]{3,2,1,0:T(8,128)(2,1)S(1)}, u32[]{:S(2)}, u32[]{:S(2)}) collective-permute-start(bf16[2,4,64,256]{3,2,1,0:T(8,128)(2,1)S(1)} %add_convert_fusion), channel_id=1, source_target_pairs={{8,0},{16,8},{24,16},{32,24},{40,32},{48,40},{56,48},{64,56},{72,6... | collective-permute-start | bytes 786440 | tf_op jit(solution)/shard_map/ppermute | solution.py:31
  169.1 12.3 %collective-permute-start.4 = (bf16[2,1,64,256]{3,2,1,0:T(8,128)(2,1)S(1)}, bf16[2,1,64,256]{3,2,1,0:T(8,128)(2,1)S(1)}, u32[]{:S(2)}, u32[]{:S(2)}) collective-permute-start(bf16[2,1,64,256]{3,2,1,0:T(8,128)(2,1)S(1)} %get-tuple-element.19), channel_id=1, source_target_pairs={{0,1},{1,2},{2,3},{3,4},{4,5},{5,6},{6,7},{8,9},{9,10},{10,11},{11... | collective-permute-start | bytes 196616 | tf_op jit(solution)/shard_map/ppermute | solution.py:19
  179.5 5.6 %collective-permute-start.5 = (bf16[2,1,64,256]{3,2,1,0:T(8,128)(2,1)S(1)}, bf16[2,1,64,256]{3,2,1,0:T(8,128)(2,1)S(1)}, u32[]{:S(2)}, u32[]{:S(2)}) collective-permute-start(bf16[2,1,64,256]{3,2,1,0:T(8,128)(2,1)S(1)} %get-tuple-element.20), channel_id=1, source_target_pairs={{1,0},{2,1},{3,2},{4,3},{5,4},{6,5},{7,6},{9,8},{10,9},{11,10},{12... | collective-permute-start | bytes 196616 | tf_op jit(solution)/shard_map/ppermute | solution.py:21
where the time goes:
time: 190 us; the launch traced here: 189 us
  waiting for transfers between devices  91.5 us (48%)
  starting transfers between devices  70.8 us (37%)
  matrix products  12 us (6%)
  local copies, waits for them, and re-layouts  11.4 us (6%)
  other arithmetic  2.37 us (1%)
    all_to_all x1, starting transfers between devices, body(): lax.all_to_all(to_groups(out_grad, groups), 'tm', split_axis=1, concat_ax...  15.4 us
    ppermute x2, starting transfers between devices, with_halo(): lax.ppermute(tail, axis, [(i, (i + 1) % count) for i in range(ends)])  14.9 us
    all_to_all x1, waiting for transfers between devices, body(): lax.all_to_all(to_groups(key_rows, groups), 'tm', split_axis=1, concat_ax...  13.3 us
    all_to_all x1, waiting for transfers between devices, body(): lax.all_to_all(to_groups(value_rows, groups), 'tm', split_axis=1, concat_...  11.8 us
    all_to_all x1, waiting for transfers between devices, body(): lax.all_to_all(to_groups(out_grad, groups), 'tm', split_axis=1, concat_ax...  11.7 us
    all_to_all x1, waiting for transfers between devices, body(): lax.all_to_all(value_grad[:, None], 'tm', split_axis=0, concat_axis=1, ti...  11.7 us
    all_to_all x1, waiting for transfers between devices, body(): lax.all_to_all(to_groups(query_rows, groups), 'tm', split_axis=1, concat_...  11.7 us
    all_to_all x1, waiting for transfers between devices, body(): lax.all_to_all(query_grad[:, None], 'tm', split_axis=0, concat_axis=1, ti...  11.4 us
  transfers between devices with their start and end apart: 13, of which 10 were waited for; matrix products, arithmetic and copies ran while one was open for 6% of the time, Pallas kernels for 0%

commit v1 on v0

v1 whole, which is shorter than its diff:
```python
import jax
import jax.numpy as jnp
from jax import lax
from jax.experimental import pallas as pl
from jax.experimental.pallas import tpu as pltpu
from jax.sharding import PartitionSpec as P

EPSILON = 1e-05
MESH = pl.DeviceIdType.MESH
BF = jnp.bfloat16
F32 = jnp.float32
T = 512
C = 256


def mm(a, b):
    return jnp.dot(a, b, preferred_element_type=F32)


def mm_nt(a, b):
    return lax.dot_general(a, b, (((1,), (1,)), ((), ())), preferred_element_type=F32)


def mm_tn(a, b):
    return lax.dot_general(a, b, (((0,), (0,)), ((), ())), preferred_element_type=F32)


def iota(shape, dim):
    return lax.broadcasted_iota(jnp.int32, shape, dim)


def to_tiles(x):
    x = x.reshape(64, 8, C)
    return jnp.concatenate([x[:, :, :128], x[:, :, 128:]], axis=1).astype(BF)


def from_tiles(x):
    x = x.astype(F32)
    return jnp.concatenate([x[:, :8], x[:, 8:]], axis=2).reshape(T, C)


def roll_rows(x, distance):
    return pltpu.roll(x, distance % x.shape[0], 0)


def kernel(
    frames_h, cot_h, ws_h, wt_h, gain_h, wq_h, wk_h, wv_h, wo_h, out_h,
    frames_v, cot_v, ws_v, wt_v, gain_v, wq_v, wk_v, wv_v, wo_v, out_v,
    halo_v, ghalo_v, gnat_v, acc0, acc1, acc2,
    fc_s, sp_s, sg_s, tg_s, fc_r, sp_r, sg_r, tg_r,
    load_sem, out_sem, hs_sem, hr_sem, s_sem, r_sem,
):
    me = lax.axis_index("tm")
    sp = lax.axis_index("space")
    z, y = me // 8, lax.rem(me, 8)
    up, down = lax.rem(sp + 7, 8), lax.rem(sp + 1, 8)

    def peer(i):
        d = i + 1
        return lax.rem(z + d // 8, 8) * 8 + lax.rem(y + lax.rem(d, 8), 8)

    pairs = [
        (frames_h, frames_v), (ws_h, ws_v), (cot_h, cot_v), (wt_h, wt_v), (gain_h, gain_v),
        (wq_h, wq_v), (wk_h, wk_v), (wv_h, wv_v), (wo_h, wo_v),
    ]
    loads = [pltpu.make_async_copy(a, b, load_sem.at[i]) for i, (a, b) in enumerate(pairs)]
    for copy in loads:
        copy.start()

    barrier = pltpu.get_barrier_semaphore()
    for other in (up, down):
        pl.semaphore_signal(barrier, inc=1, device_id=(me, other), device_id_type=MESH)

    def greet(i, carry):
        pl.semaphore_signal(barrier, inc=1, device_id=(peer(i), sp), device_id_type=MESH)
        return carry

    lax.fori_loop(0, 63, greet, 0)

    def halo_copies(src, dst, k):
        return [
            pltpu.make_async_remote_copy(
                src.at[:, row], dst.at[side], hs_sem.at[k + side], hr_sem.at[k + side],
                device_id=(me, other), device_id_type=MESH,
            )
            for side, (row, other) in enumerate(((3, down), (0, up)))
        ]

    def send_all(src, dst, k):
        def go(i, carry):
            p = peer(i)
            pltpu.make_async_remote_copy(
                src.at[p], dst.at[me], s_sem.at[k], r_sem.at[k],
                device_id=(p, sp), device_id_type=MESH,
            ).start()
            return carry

        lax.fori_loop(0, 63, go, 0)
        dst[me] = src[me]

    def wait_all(dst, sem):
        pltpu.make_async_copy(dst.at[pl.ds(0, 63)], dst.at[pl.ds(0, 63)], sem).wait()

    row_m, col_n = iota((T, T), 0), iota((T, T), 1)
    natural = (row_m // 4) % 2 * 256 + row_m // 8 * 4 + row_m % 4
    to_message = (natural == col_n).astype(F32).astype(BF)

    def taps(src, weight, pick):
        for col_tap, acc in enumerate((acc0, acc1, acc2)):
            for f in range(2):
                x = src[f].reshape(256, C)
                acc[f] = pick(x, weight, 1, col_tap)
                acc[f, 64:256] += pick(x[0:192], weight, 0, col_tap)
                acc[f, 0:192] += pick(x[64:256], weight, 2, col_tap)

    def edges(halo, weight, pick):
        keep_up = jnp.where(sp > 0, 1.0, 0.0)
        keep_down = jnp.where(sp < 7, 1.0, 0.0)
        above = halo[0].reshape(128, C)
        below = halo[1].reshape(128, C)
        for col_tap, acc in enumerate((acc0, acc1, acc2)):
            first = pick(above, weight, 0, col_tap) * keep_up
            last = pick(below, weight, 2, col_tap) * keep_down
            for f in range(2):
                acc[f, 0:64] += first[f * 64 : f * 64 + 64]
                acc[f, 192:256] += last[f * 64 : f * 64 + 64]

    def columns():
        col = iota((T, C), 0) % 64
        before = jnp.where(col == 0, 0.0, roll_rows(acc0[...].reshape(T, C), 1))
        after = jnp.where(col == 63, 0.0, roll_rows(acc2[...].reshape(T, C), -1))
        return before + acc1[...].reshape(T, C) + after

    def pick_forward(x, weight, row_tap, col_tap):
        return mm(x, weight[row_tap, col_tap])

    def pick_backward(x, weight, row_tap, col_tap):
        return mm_nt(x, weight[2 - row_tap, 2 - col_tap])

    loads[0].wait()
    loads[1].wait()
    taps(frames_v, ws_v, pick_forward)

    pl.semaphore_wait(barrier, 65)
    halos = halo_copies(frames_v, halo_v, 0)
    for copy in halos:
        copy.start()
    fc_s[:, 0:16] = to_tiles(mm(to_message, frames_v[...].reshape(T, C)))
    loads[2].wait()
    fc_s[:, 16:32] = to_tiles(mm(to_message, cot_v[...].reshape(T, C)))
    for copy in halos:
        copy.wait()
    edges(halo_v, ws_v, pick_forward)
    spatial = columns().astype(BF)
    sp_s[...] = to_tiles(mm(to_message, spatial))
    send_all(sp_s, sp_r, 1)
    send_all(fc_s, fc_r, 0)
    for copy in loads[3:]:
        copy.wait()

    wait_all(fc_r, r_sem.at[0])
    by_pixel = (row_m % 128 * 4 + row_m // 128 == col_n).astype(F32).astype(BF)
    cot_n = from_tiles(fc_r[:, 16:32]).astype(BF)
    cot_p = mm(by_pixel, cot_n).astype(BF)
    out_grad = mm_nt(cot_p, wo_v[...]).astype(BF)
    frames_n = from_tiles(fc_r[:, 0:16])
    wait_all(sp_r, r_sem.at[1])
    spatial_n = from_tiles(sp_r[...]).astype(BF)
    token = iota((T, C), 0)
    hidden_n = (
        frames_n
        + mm(spatial_n, wt_v[0])
        + jnp.where(token < 4, 0.0, roll_rows(mm(spatial_n, wt_v[1]), 4))
        + jnp.where(token < 8, 0.0, roll_rows(mm(spatial_n, wt_v[2]), 8))
    ).astype(BF)
    hidden = mm(by_pixel, hidden_n)
    gain = gain_v[...]
    inverse = lax.rsqrt(jnp.mean(hidden * hidden, axis=-1, keepdims=True) + EPSILON)
    normed = (hidden * inverse * gain).astype(BF)
    query = mm(normed, wq_v[...]).astype(BF)
    key = mm(normed, wk_v[...]).astype(BF)
    value = mm(normed, wv_v[...]).astype(BF)
    scale = 1.0 / 16.0
    causal = iota((128, 128), 1) <= iota((128, 128), 0)
    dq, dk, dv = [], [], []
    for p in range(4):
        rows = slice(p * 128, p * 128 + 128)
        q, k, v, g = query[rows], key[rows], value[rows], out_grad[rows]
        weights = jnp.where(causal, jnp.exp(mm_nt(q, k) * scale), 0.0)
        probs = weights / jnp.sum(weights, axis=-1, keepdims=True)
        prob_grad = mm_nt(g, v)
        centre = jnp.sum(probs * prob_grad, axis=-1, keepdims=True)
        score_grad = (probs * (prob_grad - centre) * scale).astype(BF)
        dv.append(mm_tn(probs.astype(BF), g).astype(BF))
        dq.append(mm(score_grad, k).astype(BF))
        dk.append(mm_tn(score_grad, q).astype(BF))
    normed_grad = (
        mm_nt(jnp.concatenate(dq, 0), wq_v[...])
        + mm_nt(jnp.concatenate(dk, 0), wk_v[...])
        + mm_nt(jnp.concatenate(dv, 0), wv_v[...])
    )
    scaled = normed_grad * gain
    mean = jnp.mean(hidden * scaled, axis=-1, keepdims=True)
    attn_grad = (inverse * scaled - hidden * (inverse * inverse * inverse) * mean).astype(BF)
    total_p = (cot_p.astype(F32) + attn_grad.astype(F32)).astype(BF)
    total_f = mm_tn(by_pixel, total_p)
    total_n = total_f.astype(BF)
    sgrad = (
        mm_nt(total_n, wt_v[0])
        + jnp.where(token >= T - 4, 0.0, roll_rows(mm_nt(total_n, wt_v[1]), -4))
        + jnp.where(token >= T - 8, 0.0, roll_rows(mm_nt(total_n, wt_v[2]), -8))
    )
    sg_s[...] = to_tiles(sgrad)
    send_all(sg_s, sg_r, 2)
    tg_s[...] = to_tiles(total_f)
    send_all(tg_s, tg_r, 3)

    wait_all(sg_r, r_sem.at[2])
    gnat_v[...] = mm_tn(to_message, from_tiles(sg_r[...]).astype(BF)).astype(BF).reshape(2, 4, 64, C)
    ghalos = halo_copies(gnat_v, ghalo_v, 2)
    for copy in ghalos:
        copy.start()
    taps(gnat_v, ws_v, pick_backward)
    for copy in ghalos:
        copy.wait()
    edges(ghalo_v, ws_v, pick_backward)
    wait_all(tg_r, r_sem.at[3])
    total = mm_tn(to_message, from_tiles(tg_r[...]).astype(BF))
    out_v[...] = (total + columns()).astype(BF).reshape(2, 4, 64, C)
    done = pltpu.make_async_copy(out_v, out_h, out_sem)
    done.start()
    for k, src in enumerate((fc_s, sp_s, sg_s, tg_s)):
        wait_all(src, s_sem.at[k])
    done.wait()


def body(frames, cotangent, w_spatial, w_temporal, norm_gain, w_query, w_key, w_value, w_out):
    big = (2, 4, 64, C)
    square = (C, C)
    vmem = pltpu.VMEM
    dma = pltpu.SemaphoreType.DMA
    message = vmem((64, 16, 128), BF)
    double = vmem((64, 32, 128), BF)
    return pl.pallas_call(
        kernel,
        out_shape=jax.ShapeDtypeStruct(big, BF),
        in_specs=[pl.BlockSpec(memory_space=pl.ANY)] * 9,
        out_specs=pl.BlockSpec(memory_space=pl.ANY),
        scratch_shapes=[
            vmem(big, BF), vmem(big, BF), vmem((3, 3, C, C), BF), vmem((3, C, C), BF), vmem((1, C), F32),
            vmem(square, BF), vmem(square, BF), vmem(square, BF), vmem(square, BF), vmem(big, BF),
            vmem((2, 2, 64, C), BF), vmem((2, 2, 64, C), BF), vmem(big, BF),
            vmem((2, 256, C), F32), vmem((2, 256, C), F32), vmem((2, 256, C), F32),
            double, message, message, message, double, message, message, message,
            dma((9,)), dma, dma((4,)), dma((4,)), dma((4,)), dma((4,)),
        ],
        compiler_params=pltpu.CompilerParams(
            collective_id=0, has_side_effects=True, vmem_limit_bytes=60 * 1024 * 1024
        ),
        name="whole",
    )(frames, cotangent, w_spatial, w_temporal, norm_gain.reshape(1, C), w_query, w_key, w_value, w_out)


def solution(mesh):
    return jax.shard_map(
        body,
        mesh=mesh,
        in_specs=(
            P("tm", "space", None, None),
            P("tm", "space", None, None),
            P(),
            P(),
            P(),
            P(),
            P(),
            P(),
            P(),
        ),
        out_specs=P("tm", "space", None, None),
        check_vma=False,
    )
```

time: 190 us -> 80.1 us (0.42)
  the two profiles are of different devices: /device:TPU:1 before, /device:TPU:5 now
where the time goes in v1:
time: 80.1 us; the launch traced here: 80 us
  Pallas kernels  78.3 us (98%)
  local copies, waits for them, and re-layouts  1.67 us (2%)
    pallas_call x1, Pallas kernels, body(): pl.pallas_call(kernel, out_shape=jax.ShapeDtypeStruct(big, BF), in_specs=...  78.3 us
    unnamed x1, local copies, waits for them, and re-layouts  1.67 us

profile of v1, /device:TPU:5, one launch (start us, length us, event | category | flops | bytes accessed | tf_op | source)
XLA Modules:
  0.0 80.0 jit_solution(3209528020890838496)
XLA Ops:
  0.0 78.3 %whole.1 = bf16[2,4,64,256]{3,2,1,0:T(8,128)(2,1)} custom-call(bf16[2,4,64,256]{3,2,1,0:T(8,128)(2,1)} %frames_h.1, bf16[2,4,64,256]{3,2,1,0:T(8,128)(2,1)} %cot_h.1, bf16[3,3,256,256]{3,2,1,0:T(8,128)(2,1)} %ws_h.1, bf16[3,256,256]{2,1,0:T(8,128)(2,1)} %wt_h.1, f32[1,256]{1,0:T(1,128)} %bitcast.1, bf16[256,256]{1,0:T(8,128)(2,1)} %wq_h.1, ...), custom_call_target="tpu_custom_call" | custom-call | tf_op jit(solution)/shard_map/whole/pallas_call | solution.py:244
  78.3 1.7 %copy.11 = bf16[2,4,64,256]{3,2,1,0:T(8,128)(2,1)} copy(bf16[2,4,64,256]{3,2,1,0:T(8,128)(2,1)} %whole.1) | data formatting | bytes 524288

commit v2 on v1

--- a/solution.py
+++ b/solution.py
@@ -44,38 +44,41 @@
 
 
 def kernel(
-    frames_h, cot_h, ws_h, wt_h, gain_h, wq_h, wk_h, wv_h, wo_h, out_h,
-    frames_v, cot_v, ws_v, wt_v, gain_v, wq_v, wk_v, wv_v, wo_v, out_v,
+    frames_h, cot_h, ws_h, wt_h, gain_h, wq_h, wk_h, wv_h, wo_h, out_v,
+    frames_v, cot_v, ws_v, wt_v, gain_v, wq_v, wk_v, wv_v, wo_v,
     halo_v, ghalo_v, gnat_v, acc0, acc1, acc2,
     fc_s, sp_s, sg_s, tg_s, fc_r, sp_r, sg_r, tg_r,
-    load_sem, out_sem, hs_sem, hr_sem, s_sem, r_sem,
+    load_sem, hs_sem, hr_sem, s_sem, r_sem, before_sem, row_sem,
 ):
     me = lax.axis_index("tm")
     sp = lax.axis_index("space")
     z, y = me // 8, lax.rem(me, 8)
     up, down = lax.rem(sp + 7, 8), lax.rem(sp + 1, 8)
 
-    def peer(i):
-        d = i + 1
-        return lax.rem(z + d // 8, 8) * 8 + lax.rem(y + lax.rem(d, 8), 8)
-
     pairs = [
-        (frames_h, frames_v), (ws_h, ws_v), (cot_h, cot_v), (wt_h, wt_v), (gain_h, gain_v),
+        (frames_h, frames_v), (cot_h, cot_v), (ws_h, ws_v), (wt_h, wt_v), (gain_h, gain_v),
         (wq_h, wq_v), (wk_h, wk_v), (wv_h, wv_v), (wo_h, wo_v),
     ]
     loads = [pltpu.make_async_copy(a, b, load_sem.at[i]) for i, (a, b) in enumerate(pairs)]
-    for copy in loads:
-        copy.start()
 
     barrier = pltpu.get_barrier_semaphore()
     for other in (up, down):
         pl.semaphore_signal(barrier, inc=1, device_id=(me, other), device_id_type=MESH)
 
-    def greet(i, carry):
-        pl.semaphore_signal(barrier, inc=1, device_id=(peer(i), sp), device_id_type=MESH)
-        return carry
-
-    lax.fori_loop(0, 63, greet, 0)
+    @pl.when(z > 0)
+    def _():
+        pl.semaphore_signal(barrier, inc=1, device_id=(me - 8, sp), device_id_type=MESH)
+
+    for j in range(1, 8):
+        p = z * 8 + lax.rem(y + j, 8)
+        pl.semaphore_signal(barrier, inc=1, device_id=(p, sp), device_id_type=MESH)
+
+    @pl.when(z < 7)
+    def _():
+        pl.semaphore_signal(barrier, inc=1, device_id=(me + 8, sp), device_id_type=MESH)
+
+    for copy in loads:
+        copy.start()
 
     def halo_copies(src, dst, k):
         return [
@@ -86,16 +89,31 @@
             for side, (row, other) in enumerate(((3, down), (0, up)))
         ]
 
-    def send_all(src, dst, k):
-        def go(i, carry):
-            p = peer(i)
+    def send_row(src, dst, k, row, others=8):
+        for j in range(8 - others, 8):
+            p = row * 8 + lax.rem(y + j, 8)
             pltpu.make_async_remote_copy(
                 src.at[p], dst.at[me], s_sem.at[k], r_sem.at[k],
                 device_id=(p, sp), device_id_type=MESH,
             ).start()
+
+    def send_before(src, dst, k):
+        send_row(src, dst, k, z, 7)
+
+        def go(i, carry):
+            send_row(src, dst, k, z - i)
             return carry
 
-        lax.fori_loop(0, 63, go, 0)
+        lax.fori_loop(1, z + 1, go, 0)
+        dst[me] = src[me]
+
+    def send_all(src, dst, k):
+        def go(i, carry):
+            send_row(src, dst, k, lax.rem(z + i, 8))
+            return carry
+
+        lax.fori_loop(1, 8, go, 0)
+        send_row(src, dst, k, z, 7)
         dst[me] = src[me]
 
     def wait_all(dst, sem):
@@ -137,24 +155,49 @@
     def pick_backward(x, weight, row_tap, col_tap):
         return mm_nt(x, weight[2 - row_tap, 2 - col_tap])
 
-    loads[0].wait()
-    loads[1].wait()
-    taps(frames_v, ws_v, pick_forward)
-
-    pl.semaphore_wait(barrier, 65)
-    halos = halo_copies(frames_v, halo_v, 0)
+    met = 9 + jnp.where(z > 0, 1, 0) + jnp.where(z < 7, 1, 0)
+    pl.semaphore_wait(barrier, met)
+    halos = halo_copies(frames_h, halo_v, 0)
     for copy in halos:
         copy.start()
+
+    @pl.when(z > 0)
+    def _():
+        pl.semaphore_wait(before_sem, 1)
+
+    @pl.when(z < 7)
+    def _():
+        pl.semaphore_signal(before_sem, inc=1, device_id=(me + 8, sp), device_id_type=MESH)
+
+    def tell(i, carry):
+        pl.semaphore_signal(
+            row_sem.at[z], inc=1, device_id=((z - i) * 8 + y, sp), device_id_type=MESH
+        )
+        return carry
+
+    lax.fori_loop(1, z + 1, tell, 0)
+
+    loads[0].wait()
     fc_s[:, 0:16] = to_tiles(mm(to_message, frames_v[...].reshape(T, C)))
+    loads[1].wait()
+    fc_s[:, 16:32] = to_tiles(mm(to_message, cot_v[...].reshape(T, C)))
+    send_before(fc_s, fc_r, 0)
     loads[2].wait()
-    fc_s[:, 16:32] = to_tiles(mm(to_message, cot_v[...].reshape(T, C)))
+    taps(frames_v, ws_v, pick_forward)
     for copy in halos:
         copy.wait()
     edges(halo_v, ws_v, pick_forward)
     spatial = columns().astype(BF)
     sp_s[...] = to_tiles(mm(to_message, spatial))
-    send_all(sp_s, sp_r, 1)
-    send_all(fc_s, fc_r, 0)
+    send_before(sp_s, sp_r, 1)
+
+    def later(row, carry):
+        pl.semaphore_wait(row_sem.at[row], 1)
+        send_row(fc_s, fc_r, 0, row)
+        send_row(sp_s, sp_r, 1, row)
+        return carry
+
+    lax.fori_loop(z + 1, 8, later, 0)
     for copy in loads[3:]:
         copy.wait()
 
@@ -213,6 +256,7 @@
     sg_s[...] = to_tiles(sgrad)
     send_all(sg_s, sg_r, 2)
     tg_s[...] = to_tiles(total_f)
+    wait_all(sg_s, s_sem.at[2])
     send_all(tg_s, tg_r, 3)
 
     wait_all(sg_r, r_sem.at[2])
@@ -227,11 +271,8 @@
     wait_all(tg_r, r_sem.at[3])
     total = mm_tn(to_message, from_tiles(tg_r[...]).astype(BF))
     out_v[...] = (total + columns()).astype(BF).reshape(2, 4, 64, C)
-    done = pltpu.make_async_copy(out_v, out_h, out_sem)
-    done.start()
-    for k, src in enumerate((fc_s, sp_s, sg_s, tg_s)):
+    for k, src in ((0, fc_s), (1, sp_s), (3, tg_s)):
         wait_all(src, s_sem.at[k])
-    done.wait()
 
 
 def body(frames, cotangent, w_spatial, w_temporal, norm_gain, w_query, w_key, w_value, w_out):
@@ -245,17 +286,18 @@
         kernel,
         out_shape=jax.ShapeDtypeStruct(big, BF),
         in_specs=[pl.BlockSpec(memory_space=pl.ANY)] * 9,
-        out_specs=pl.BlockSpec(memory_space=pl.ANY),
+        out_specs=pl.BlockSpec(memory_space=pltpu.VMEM),
         scratch_shapes=[
             vmem(big, BF), vmem(big, BF), vmem((3, 3, C, C), BF), vmem((3, C, C), BF), vmem((1, C), F32),
-            vmem(square, BF), vmem(square, BF), vmem(square, BF), vmem(square, BF), vmem(big, BF),
+            vmem(square, BF), vmem(square, BF), vmem(square, BF), vmem(square, BF),
             vmem((2, 2, 64, C), BF), vmem((2, 2, 64, C), BF), vmem(big, BF),
             vmem((2, 256, C), F32), vmem((2, 256, C), F32), vmem((2, 256, C), F32),
             double, message, message, message, double, message, message, message,
-            dma((9,)), dma, dma((4,)), dma((4,)), dma((4,)), dma((4,)),
+            dma((9,)), dma((4,)), dma((4,)), dma((4,)), dma((4,)),
+            pltpu.SemaphoreType.REGULAR, pltpu.SemaphoreType.REGULAR((8,)),
         ],
         compiler_params=pltpu.CompilerParams(
-            collective_id=0, has_side_effects=True, vmem_limit_bytes=60 * 1024 * 1024
+            collective_id=0, has_side_effects=True, vmem_limit_bytes=56 * 1024 * 1024
         ),
         name="whole",
     )(frames, cotangent, w_spatial, w_temporal, norm_gain.reshape(1, C), w_query, w_key, w_value, w_out)

time: 80.1 us -> 67.2 us (0.84)
  the two profiles are of different devices: /device:TPU:5 before, /device:TPU:1 now
where the time goes in v2:
time: 67.2 us; the launch traced here: 67 us
  Pallas kernels  65.4 us (97%)
  local copies, waits for them, and re-layouts  1.67 us (2%)
    pallas_call x1, Pallas kernels, body(): pl.pallas_call(kernel, out_shape=jax.ShapeDtypeStruct(big, BF), in_specs=...  65.4 us
    unnamed x1, local copies, waits for them, and re-layouts  1.67 us

profile of v2, /device:TPU:1, one launch (start us, length us, event | category | flops | bytes accessed | tf_op | source)
XLA Modules:
  0.0 67.0 jit_solution(11354467942112849379)
XLA Ops:
  0.0 65.4 %whole.1 = bf16[2,4,64,256]{3,2,1,0:T(8,128)(2,1)} custom-call(bf16[2,4,64,256]{3,2,1,0:T(8,128)(2,1)} %frames_h.1, bf16[2,4,64,256]{3,2,1,0:T(8,128)(2,1)} %cot_h.1, bf16[3,3,256,256]{3,2,1,0:T(8,128)(2,1)} %ws_h.1, bf16[3,256,256]{2,1,0:T(8,128)(2,1)} %wt_h.1, f32[1,256]{1,0:T(1,128)} %bitcast.1, bf16[256,256]{1,0:T(8,128)(2,1)} %wq_h.1, ...), custom_call_target="tpu_custom_call" | custom-call | tf_op jit(solution)/shard_map/whole/pallas_call | solution.py:285
  65.4 1.7 %copy.11 = bf16[2,4,64,256]{3,2,1,0:T(8,128)(2,1)} copy(bf16[2,4,64,256]{3,2,1,0:T(8,128)(2,1)} %whole.1) | data formatting | bytes 524288

commit v3 on v2

--- a/solution.py
+++ b/solution.py
@@ -46,9 +46,9 @@
 def kernel(
     frames_h, cot_h, ws_h, wt_h, gain_h, wq_h, wk_h, wv_h, wo_h, out_v,
     frames_v, cot_v, ws_v, wt_v, gain_v, wq_v, wk_v, wv_v, wo_v,
-    halo_v, ghalo_v, gnat_v, acc0, acc1, acc2,
-    fc_s, sp_s, sg_s, tg_s, fc_r, sp_r, sg_r, tg_r,
-    load_sem, hs_sem, hr_sem, s_sem, r_sem, before_sem, row_sem,
+    halo_v, ghalo_v, gnat_v, spat_v, prev_v, acc0, acc1, acc2,
+    ct_s, hd_s, sg_s, tg_s, ct_r, hd_r, sg_r, tg_r,
+    load_sem, hs_sem, hr_sem, s_sem, r_sem, fs_sem, fr_sem, before_sem, row_sem,
 ):
     me = lax.axis_index("tm")
     sp = lax.axis_index("space")
@@ -76,6 +76,10 @@
     @pl.when(z < 7)
     def _():
         pl.semaphore_signal(barrier, inc=1, device_id=(me + 8, sp), device_id_type=MESH)
+
+    @pl.when(jnp.logical_and(y == 0, z > 0))
+    def _():
+        pl.semaphore_signal(barrier, inc=1, device_id=(me - 1, sp), device_id_type=MESH)
 
     for copy in loads:
         copy.start()
@@ -114,6 +118,16 @@
 
         lax.fori_loop(1, 8, go, 0)
         send_row(src, dst, k, z, 7)
+        dst[me] = src[me]
+
+    def send_ascending(src, dst, k):
+        def go(i, carry):
+            send_row(src, dst, k, i)
+            return carry
+
+        lax.fori_loop(0, z, go, 0)
+        send_row(src, dst, k, z, 7)
+        lax.fori_loop(z + 1, 8, go, 0)
         dst[me] = src[me]
 
     def wait_all(dst, sem):
@@ -143,11 +157,12 @@
                 acc[f, 0:64] += first[f * 64 : f * 64 + 64]
                 acc[f, 192:256] += last[f * 64 : f * 64 + 64]
 
-    def columns():
-        col = iota((T, C), 0) % 64
-        before = jnp.where(col == 0, 0.0, roll_rows(acc0[...].reshape(T, C), 1))
-        after = jnp.where(col == 63, 0.0, roll_rows(acc2[...].reshape(T, C), -1))
-        return before + acc1[...].reshape(T, C) + after
+    def columns(f, low, high):
+        rows = slice(low * 64, high * 64)
+        col = iota(((high - low) * 64, C), 0) % 64
+        before = jnp.where(col == 0, 0.0, roll_rows(acc0[f, rows], 1))
+        after = jnp.where(col == 63, 0.0, roll_rows(acc2[f, rows], -1))
+        return before + acc1[f, rows] + after
 
     def pick_forward(x, weight, row_tap, col_tap):
         return mm(x, weight[row_tap, col_tap])
@@ -156,10 +171,33 @@
         return mm_nt(x, weight[2 - row_tap, 2 - col_tap])
 
     met = 9 + jnp.where(z > 0, 1, 0) + jnp.where(z < 7, 1, 0)
+    met += jnp.where(jnp.logical_and(y == 7, z < 7), 1, 0)
     pl.semaphore_wait(barrier, met)
     halos = halo_copies(frames_h, halo_v, 0)
     for copy in halos:
         copy.start()
+
+    def frame_copy(part, rows):
+        return pltpu.make_async_remote_copy(
+            spat_v.at[:, rows], prev_v.at[:, rows], fs_sem.at[part], fr_sem.at[part],
+            device_id=(me + 1, sp), device_id_type=MESH,
+        )
+
+    shifts = [frame_copy(0, pl.ds(1, 2)), frame_copy(1, pl.ds(0, 1)), frame_copy(2, pl.ds(3, 1))]
+
+    def spatial_rows(low, high):
+        for f in range(2):
+            rows = columns(f, low, high).astype(BF)
+            spat_v[f, low:high] = rows.reshape(high - low, 64, C)
+
+    loads[0].wait()
+    loads[2].wait()
+    taps(frames_v, ws_v, pick_forward)
+    spatial_rows(1, 3)
+
+    @pl.when(me < 63)
+    def _():
+        shifts[0].start()
 
     @pl.when(z > 0)
     def _():
@@ -177,46 +215,61 @@
 
     lax.fori_loop(1, z + 1, tell, 0)
 
-    loads[0].wait()
-    fc_s[:, 0:16] = to_tiles(mm(to_message, frames_v[...].reshape(T, C)))
-    loads[1].wait()
-    fc_s[:, 16:32] = to_tiles(mm(to_message, cot_v[...].reshape(T, C)))
-    send_before(fc_s, fc_r, 0)
-    loads[2].wait()
-    taps(frames_v, ws_v, pick_forward)
     for copy in halos:
         copy.wait()
     edges(halo_v, ws_v, pick_forward)
-    spatial = columns().astype(BF)
-    sp_s[...] = to_tiles(mm(to_message, spatial))
-    send_before(sp_s, sp_r, 1)
-
-    def later(row, carry):
-        pl.semaphore_wait(row_sem.at[row], 1)
-        send_row(fc_s, fc_r, 0, row)
-        send_row(sp_s, sp_r, 1, row)
-        return carry
-
-    lax.fori_loop(z + 1, 8, later, 0)
+    spatial_rows(0, 1)
+    spatial_rows(3, 4)
+
+    @pl.when(me < 63)
+    def _():
+        shifts[1].start()
+        shifts[2].start()
+
+    loads[1].wait()
+    ct_s[...] = to_tiles(mm(to_message, cot_v[...].reshape(T, C)))
+    send_before(ct_s, ct_r, 0)
     for copy in loads[3:]:
         copy.wait()
-
-    wait_all(fc_r, r_sem.at[0])
+    now = [spat_v[f].reshape(256, C) for f in range(2)]
+    acc0[0] = frames_v[0].reshape(256, C).astype(F32) + mm(now[0], wt_v[0])
+    acc0[1] = frames_v[1].reshape(256, C).astype(F32) + mm(now[1], wt_v[0]) + mm(now[0], wt_v[1])
+    def later_cot(row, carry):
+        pl.semaphore_wait(row_sem.at[row], 1)
+        send_row(ct_s, ct_r, 0, row)
+        return carry
+
+    lax.fori_loop(z + 1, 8, later_cot, 0)
+
+    @pl.when(me > 0)
+    def _():
+        for copy in shifts:
+            copy.wait_recv()
+
+    @pl.when(me == 0)
+    def _():
+        prev_v[...] = jnp.zeros_like(prev_v)
+
+    past = [prev_v[f].reshape(256, C) for f in range(2)]
+    acc0[0] += mm(past[1], wt_v[1]) + mm(past[0], wt_v[2])
+    acc0[1] += mm(past[1], wt_v[2])
+    hd_s[...] = to_tiles(mm(to_message, acc0[...].reshape(T, C).astype(BF)))
+    send_before(hd_s, hd_r, 1)
+
+    def later(row, carry):
+        send_row(hd_s, hd_r, 1, row)
+        return carry
+
+    lax.fori_loop(z + 1, 8, later, 0)
+
+    wait_all(ct_r, r_sem.at[0])
     by_pixel = (row_m % 128 * 4 + row_m // 128 == col_n).astype(F32).astype(BF)
-    cot_n = from_tiles(fc_r[:, 16:32]).astype(BF)
+    cot_n = from_tiles(ct_r[...]).astype(BF)
     cot_p = mm(by_pixel, cot_n).astype(BF)
     out_grad = mm_nt(cot_p, wo_v[...]).astype(BF)
-    frames_n = from_tiles(fc_r[:, 0:16])
-    wait_all(sp_r, r_sem.at[1])
-    spatial_n = from_tiles(sp_r[...]).astype(BF)
+    wait_all(hd_r, r_sem.at[1])
     token = iota((T, C), 0)
-    hidden_n = (
-        frames_n
-        + mm(spatial_n, wt_v[0])
-        + jnp.where(token < 4, 0.0, roll_rows(mm(spatial_n, wt_v[1]), 4))
-        + jnp.where(token < 8, 0.0, roll_rows(mm(spatial_n, wt_v[2]), 8))
-    ).astype(BF)
-    hidden = mm(by_pixel, hidden_n)
+    hidden = mm(by_pixel, from_tiles(hd_r[...]).astype(BF))
     gain = gain_v[...]
     inverse = lax.rsqrt(jnp.mean(hidden * hidden, axis=-1, keepdims=True) + EPSILON)
     normed = (hidden * inverse * gain).astype(BF)
@@ -254,10 +307,10 @@
         + jnp.where(token >= T - 8, 0.0, roll_rows(mm_nt(total_n, wt_v[2]), -8))
     )
     sg_s[...] = to_tiles(sgrad)
-    send_all(sg_s, sg_r, 2)
+    send_ascending(sg_s, sg_r, 2)
     tg_s[...] = to_tiles(total_f)
     wait_all(sg_s, s_sem.at[2])
-    send_all(tg_s, tg_r, 3)
+    send_ascending(tg_s, tg_r, 3)
 
     wait_all(sg_r, r_sem.at[2])
     gnat_v[...] = mm_tn(to_message, from_tiles(sg_r[...]).astype(BF)).astype(BF).reshape(2, 4, 64, C)
@@ -270,8 +323,15 @@
     edges(ghalo_v, ws_v, pick_backward)
     wait_all(tg_r, r_sem.at[3])
     total = mm_tn(to_message, from_tiles(tg_r[...]).astype(BF))
-    out_v[...] = (total + columns()).astype(BF).reshape(2, 4, 64, C)
-    for k, src in ((0, fc_s), (1, sp_s), (3, tg_s)):
+    for f in range(2):
+        out_v[f] = (total[f * 256 : f * 256 + 256] + columns(f, 0, 4)).astype(BF).reshape(4, 64, C)
+
+    @pl.when(me < 63)
+    def _():
+        for copy in shifts:
+            copy.wait_send()
+
+    for k, src in ((0, ct_s), (1, hd_s), (3, tg_s)):
         wait_all(src, s_sem.at[k])
 
 
@@ -281,7 +341,8 @@
     vmem = pltpu.VMEM
     dma = pltpu.SemaphoreType.DMA
     message = vmem((64, 16, 128), BF)
-    double = vmem((64, 32, 128), BF)
+    arrays = (frames, cotangent, w_spatial, w_temporal, norm_gain.reshape(1, C), w_query, w_key, w_value, w_out)
+    arrays = [pltpu.with_memory_space_constraint(a, pltpu.HBM) for a in arrays]
     return pl.pallas_call(
         kernel,
         out_shape=jax.ShapeDtypeStruct(big, BF),
@@ -290,17 +351,17 @@
         scratch_shapes=[
             vmem(big, BF), vmem(big, BF), vmem((3, 3, C, C), BF), vmem((3, C, C), BF), vmem((1, C), F32),
             vmem(square, BF), vmem(square, BF), vmem(square, BF), vmem(square, BF),
-            vmem((2, 2, 64, C), BF), vmem((2, 2, 64, C), BF), vmem(big, BF),
+            vmem((2, 2, 64, C), BF), vmem((2, 2, 64, C), BF), vmem(big, BF), vmem(big, BF), vmem(big, BF),
             vmem((2, 256, C), F32), vmem((2, 256, C), F32), vmem((2, 256, C), F32),
-            double, message, message, message, double, message, message, message,
-            dma((9,)), dma((4,)), dma((4,)), dma((4,)), dma((4,)),
+            message, message, message, message, message, message, message, message,
+            dma((9,)), dma((4,)), dma((4,)), dma((4,)), dma((4,)), dma((3,)), dma((3,)),
             pltpu.SemaphoreType.REGULAR, pltpu.SemaphoreType.REGULAR((8,)),
         ],
         compiler_params=pltpu.CompilerParams(
-            collective_id=0, has_side_effects=True, vmem_limit_bytes=56 * 1024 * 1024
+            collective_id=0, has_side_effects=True, vmem_limit_bytes=48 * 1024 * 1024
         ),
         name="whole",
-    )(frames, cotangent, w_spatial, w_temporal, norm_gain.reshape(1, C), w_query, w_key, w_value, w_out)
+    )(*arrays)
 
 
 def solution(mesh):

time: 67.2 us -> 55.8 us (0.83)
  the two profiles are of different devices: /device:TPU:1 before, /device:TPU:64 now
where the time goes in v3:
time: 55.8 us; the launch traced here: 55.7 us
  Pallas kernels  55 us (99%)
  local copies, waits for them, and re-layouts  0.71 us (1%)
    pallas_call x1, Pallas kernels, body(): pl.pallas_call(kernel, out_shape=jax.ShapeDtypeStruct(big, BF), in_specs=...  55 us

profile of v3, /device:TPU:64, one launch (start us, length us, event | category | flops | bytes accessed | tf_op | source)
XLA Modules:
  0.0 55.7 jit_solution(17683541613484291511)
XLA Ops:
  0.0 55.0 %whole.1 = bf16[2,4,64,256]{3,2,1,0:T(8,128)(2,1)S(1)} custom-call(bf16[2,4,64,256]{3,2,1,0:T(8,128)(2,1)} %frames_h.1, bf16[2,4,64,256]{3,2,1,0:T(8,128)(2,1)} %cot_h.1, bf16[3,3,256,256]{3,2,1,0:T(8,128)(2,1)} %ws_h.1, bf16[3,256,256]{2,1,0:T(8,128)(2,1)} %wt_h.1, f32[1,256]{1,0:T(1,128)} %bitcast.1, bf16[256,256]{1,0:T(8,128)(2,1)} %wq_h.1, ...), custom_call_target="tpu_custom_call" | custom-call | tf_op jit(solution)/shard_map/whole/pallas_call | solution.py:346
  55.0 0.7 %copy.11 = bf16[2,4,64,256]{3,2,1,0:T(8,128)(2,1)} copy(bf16[2,4,64,256]{3,2,1,0:T(8,128)(2,1)S(1)} %whole.1) | data formatting | bytes 524288

commit v4 on v3

--- a/solution.py
+++ b/solution.py
@@ -47,7 +47,7 @@
     frames_h, cot_h, ws_h, wt_h, gain_h, wq_h, wk_h, wv_h, wo_h, out_v,
     frames_v, cot_v, ws_v, wt_v, gain_v, wq_v, wk_v, wv_v, wo_v,
     halo_v, ghalo_v, gnat_v, spat_v, prev_v, acc0, acc1, acc2,
-    ct_s, hd_s, sg_s, tg_s, ct_r, hd_r, sg_r, tg_r,
+    ct_s, hd_s, sg_s, tg_s, ct_r, hd_r, sg_r, tg_r, to_msg_v, from_msg_v, by_pixel_v, by_frame_v,
     load_sem, hs_sem, hr_sem, s_sem, r_sem, fs_sem, fr_sem, before_sem, row_sem,
 ):
     me = lax.axis_index("tm")
@@ -134,8 +134,17 @@
         pltpu.make_async_copy(dst.at[pl.ds(0, 63)], dst.at[pl.ds(0, 63)], sem).wait()
 
     row_m, col_n = iota((T, T), 0), iota((T, T), 1)
-    natural = (row_m // 4) % 2 * 256 + row_m // 8 * 4 + row_m % 4
-    to_message = (natural == col_n).astype(F32).astype(BF)
+
+    def natural(token):
+        return token // 4 % 2 * 256 + token // 8 * 4 + token % 4
+
+    def of_pixel(token):
+        return token % 128 * 4 + token // 128
+
+    def one_hot(wanted, other):
+        return (wanted == other).astype(F32).astype(BF)
+
+    to_msg_v[...] = one_hot(natural(row_m), col_n)
 
     def taps(src, weight, pick):
         for col_tap, acc in enumerate((acc0, acc1, acc2)):
@@ -227,7 +236,7 @@
         shifts[2].start()
 
     loads[1].wait()
-    ct_s[...] = to_tiles(mm(to_message, cot_v[...].reshape(T, C)))
+    ct_s[...] = to_tiles(mm(to_msg_v[...], cot_v[...].reshape(T, C)))
     send_before(ct_s, ct_r, 0)
     for copy in loads[3:]:
         copy.wait()
@@ -253,7 +262,7 @@
     past = [prev_v[f].reshape(256, C) for f in range(2)]
     acc0[0] += mm(past[1], wt_v[1]) + mm(past[0], wt_v[2])
     acc0[1] += mm(past[1], wt_v[2])
-    hd_s[...] = to_tiles(mm(to_message, acc0[...].reshape(T, C).astype(BF)))
+    hd_s[...] = to_tiles(mm(to_msg_v[...], acc0[...].reshape(T, C).astype(BF)))
     send_before(hd_s, hd_r, 1)
 
     def later(row, carry):
@@ -262,14 +271,16 @@
 
     lax.fori_loop(z + 1, 8, later, 0)
 
+    from_msg_v[...] = one_hot(natural(col_n), row_m)
+    by_pixel_v[...] = one_hot(of_pixel(row_m), col_n)
+    by_frame_v[...] = one_hot(of_pixel(col_n), row_m)
     wait_all(ct_r, r_sem.at[0])
-    by_pixel = (row_m % 128 * 4 + row_m // 128 == col_n).astype(F32).astype(BF)
     cot_n = from_tiles(ct_r[...]).astype(BF)
-    cot_p = mm(by_pixel, cot_n).astype(BF)
+    cot_p = mm(by_pixel_v[...], cot_n).astype(BF)
     out_grad = mm_nt(cot_p, wo_v[...]).astype(BF)
     wait_all(hd_r, r_sem.at[1])
     token = iota((T, C), 0)
-    hidden = mm(by_pixel, from_tiles(hd_r[...]).astype(BF))
+    hidden = mm(by_pixel_v[...], from_tiles(hd_r[...]).astype(BF))
     gain = gain_v[...]
     inverse = lax.rsqrt(jnp.mean(hidden * hidden, axis=-1, keepdims=True) + EPSILON)
     normed = (hidden * inverse * gain).astype(BF)
@@ -278,18 +289,18 @@
     value = mm(normed, wv_v[...]).astype(BF)
     scale = 1.0 / 16.0
     causal = iota((128, 128), 1) <= iota((128, 128), 0)
-    dq, dk, dv = [], [], []
-    for p in range(4):
-        rows = slice(p * 128, p * 128 + 128)
-        q, k, v, g = query[rows], key[rows], value[rows], out_grad[rows]
-        weights = jnp.where(causal, jnp.exp(mm_nt(q, k) * scale), 0.0)
-        probs = weights / jnp.sum(weights, axis=-1, keepdims=True)
-        prob_grad = mm_nt(g, v)
-        centre = jnp.sum(probs * prob_grad, axis=-1, keepdims=True)
-        score_grad = (probs * (prob_grad - centre) * scale).astype(BF)
-        dv.append(mm_tn(probs.astype(BF), g).astype(BF))
-        dq.append(mm(score_grad, k).astype(BF))
-        dk.append(mm_tn(score_grad, q).astype(BF))
+    parts = [slice(p * 128, p * 128 + 128) for p in range(4)]
+    scores = [mm_nt(query[r], key[r]) for r in parts]
+    prob_grad = [mm_nt(out_grad[r], value[r]) for r in parts]
+    weights = [jnp.where(causal, jnp.exp(x * scale), 0.0) for x in scores]
+    probs = [w / jnp.sum(w, axis=-1, keepdims=True) for w in weights]
+    centre = [jnp.sum(p * g, axis=-1, keepdims=True) for p, g in zip(probs, prob_grad)]
+    score_grad = [
+        (p * (g - c) * scale).astype(BF) for p, g, c in zip(probs, prob_grad, centre)
+    ]
+    dv = [mm_tn(p.astype(BF), out_grad[r]).astype(BF) for p, r in zip(probs, parts)]
+    dq = [mm(g, key[r]).astype(BF) for g, r in zip(score_grad, parts)]
+    dk = [mm_tn(g, query[r]).astype(BF) for g, r in zip(score_grad, parts)]
     normed_grad = (
         mm_nt(jnp.concatenate(dq, 0), wq_v[...])
         + mm_nt(jnp.concatenate(dk, 0), wk_v[...])
@@ -299,7 +310,7 @@
     mean = jnp.mean(hidden * scaled, axis=-1, keepdims=True)
     attn_grad = (inverse * scaled - hidden * (inverse * inverse * inverse) * mean).astype(BF)
     total_p = (cot_p.astype(F32) + attn_grad.astype(F32)).astype(BF)
-    total_f = mm_tn(by_pixel, total_p)
+    total_f = mm(by_frame_v[...], total_p)
     total_n = total_f.astype(BF)
     sgrad = (
         mm_nt(total_n, wt_v[0])
@@ -313,7 +324,7 @@
     send_ascending(tg_s, tg_r, 3)
 
     wait_all(sg_r, r_sem.at[2])
-    gnat_v[...] = mm_tn(to_message, from_tiles(sg_r[...]).astype(BF)).astype(BF).reshape(2, 4, 64, C)
+    gnat_v[...] = mm(from_msg_v[...], from_tiles(sg_r[...]).astype(BF)).astype(BF).reshape(2, 4, 64, C)
     ghalos = halo_copies(gnat_v, ghalo_v, 2)
     for copy in ghalos:
         copy.start()
@@ -322,7 +333,7 @@
         copy.wait()
     edges(ghalo_v, ws_v, pick_backward)
     wait_all(tg_r, r_sem.at[3])
-    total = mm_tn(to_message, from_tiles(tg_r[...]).astype(BF))
+    total = mm(from_msg_v[...], from_tiles(tg_r[...]).astype(BF))
     for f in range(2):
         out_v[f] = (total[f * 256 : f * 256 + 256] + columns(f, 0, 4)).astype(BF).reshape(4, 64, C)
 
@@ -354,6 +365,7 @@
             vmem((2, 2, 64, C), BF), vmem((2, 2, 64, C), BF), vmem(big, BF), vmem(big, BF), vmem(big, BF),
             vmem((2, 256, C), F32), vmem((2, 256, C), F32), vmem((2, 256, C), F32),
             message, message, message, message, message, message, message, message,
+            vmem((T, T), BF), vmem((T, T), BF), vmem((T, T), BF), vmem((T, T), BF),
             dma((9,)), dma((4,)), dma((4,)), dma((4,)), dma((4,)), dma((3,)), dma((3,)),
             pltpu.SemaphoreType.REGULAR, pltpu.SemaphoreType.REGULAR((8,)),
         ],

time: 55.8 us -> 55 us (0.986)
  Pallas kernels: 55 us -> 54.1 us
    pallas_call x1, Pallas kernels: 55 us -> 54.1 us  [body(): pl.pallas_call(kernel, out_shape=jax.ShapeDtypeStruct(big, BF), in_specs=...]
where the time goes in v4:
time: 55 us; the launch traced here: 54.8 us
  Pallas kernels  54.1 us (98%)
  local copies, waits for them, and re-layouts  0.71 us (1%)
    pallas_call x1, Pallas kernels, body(): pl.pallas_call(kernel, out_shape=jax.ShapeDtypeStruct(big, BF), in_specs=...  54.1 us

profile of v4, /device:TPU:64, one launch (start us, length us, event | category | flops | bytes accessed | tf_op | source)
XLA Modules:
  0.0 54.8 jit_solution(16511688242015934530)
XLA Ops:
  0.0 54.1 %whole.1 = bf16[2,4,64,256]{3,2,1,0:T(8,128)(2,1)S(1)} custom-call(bf16[2,4,64,256]{3,2,1,0:T(8,128)(2,1)} %frames_h.1, bf16[2,4,64,256]{3,2,1,0:T(8,128)(2,1)} %cot_h.1, bf16[3,3,256,256]{3,2,1,0:T(8,128)(2,1)} %ws_h.1, bf16[3,256,256]{2,1,0:T(8,128)(2,1)} %wt_h.1, f32[1,256]{1,0:T(1,128)} %bitcast.1, bf16[256,256]{1,0:T(8,128)(2,1)} %wq_h.1, ...), custom_call_target="tpu_custom_call" | custom-call | tf_op jit(solution)/shard_map/whole/pallas_call | solution.py:357
  54.1 0.7 %copy.11 = bf16[2,4,64,256]{3,2,1,0:T(8,128)(2,1)} copy(bf16[2,4,64,256]{3,2,1,0:T(8,128)(2,1)S(1)} %whole.1) | data formatting | bytes 524288

commit v5 on v4

--- a/solution.py
+++ b/solution.py
@@ -36,7 +36,7 @@
 
 def from_tiles(x):
     x = x.astype(F32)
-    return jnp.concatenate([x[:, :8], x[:, 8:]], axis=2).reshape(T, C)
+    return jnp.concatenate([x[:, :8], x[:, 8:]], axis=2).reshape(-1, C)
 
 
 def roll_rows(x, distance):
@@ -93,19 +93,19 @@
             for side, (row, other) in enumerate(((3, down), (0, up)))
         ]
 
-    def send_row(src, dst, k, row, others=8):
+    def send_row(src, dst, k, row, others=8, r=None):
         for j in range(8 - others, 8):
             p = row * 8 + lax.rem(y + j, 8)
             pltpu.make_async_remote_copy(
-                src.at[p], dst.at[me], s_sem.at[k], r_sem.at[k],
+                src.at[p], dst.at[me], s_sem.at[k], r_sem.at[k if r is None else r],
                 device_id=(p, sp), device_id_type=MESH,
             ).start()
 
-    def send_before(src, dst, k):
-        send_row(src, dst, k, z, 7)
+    def send_before(src, dst, k, r=None):
+        send_row(src, dst, k, z, 7, r)
 
         def go(i, carry):
-            send_row(src, dst, k, z - i)
+            send_row(src, dst, k, z - i, 8, r)
             return carry
 
         lax.fori_loop(1, z + 1, go, 0)
@@ -139,7 +139,7 @@
         return token // 4 % 2 * 256 + token // 8 * 4 + token % 4
 
     def of_pixel(token):
-        return token % 128 * 4 + token // 128
+        return token % 64 * 4 + token // 64
 
     def one_hot(wanted, other):
         return (wanted == other).astype(F32).astype(BF)
@@ -263,54 +263,89 @@
     acc0[0] += mm(past[1], wt_v[1]) + mm(past[0], wt_v[2])
     acc0[1] += mm(past[1], wt_v[2])
     hd_s[...] = to_tiles(mm(to_msg_v[...], acc0[...].reshape(T, C).astype(BF)))
-    send_before(hd_s, hd_r, 1)
+    half = jnp.where(z < 4, 1, 4)
+    send_before(hd_s, hd_r, 1, half)
 
     def later(row, carry):
-        send_row(hd_s, hd_r, 1, row)
+        send_row(hd_s, hd_r, 1, row, 8, half)
         return carry
 
     lax.fori_loop(z + 1, 8, later, 0)
 
     from_msg_v[...] = one_hot(natural(col_n), row_m)
-    by_pixel_v[...] = one_hot(of_pixel(row_m), col_n)
-    by_frame_v[...] = one_hot(of_pixel(col_n), row_m)
+    row_h, col_h = iota((T // 2, T // 2), 0), iota((T // 2, T // 2), 1)
+    by_pixel_v[...] = one_hot(of_pixel(row_h), col_h)
+    by_frame_v[...] = one_hot(of_pixel(col_h), row_h)
     wait_all(ct_r, r_sem.at[0])
     cot_n = from_tiles(ct_r[...]).astype(BF)
-    cot_p = mm(by_pixel_v[...], cot_n).astype(BF)
+    cot_p = jnp.concatenate(
+        [mm(by_pixel_v[...], cot_n[:256]), mm(by_pixel_v[...], cot_n[256:])], 0
+    ).astype(BF)
     out_grad = mm_nt(cot_p, wo_v[...]).astype(BF)
-    wait_all(hd_r, r_sem.at[1])
+    gain = gain_v[...]
+
+    def wait_half(k, mine):
+        def some(count):
+            part = hd_r.at[pl.ds(0, count)]
+            pltpu.make_async_copy(part, part, r_sem.at[k]).wait()
+
+        @pl.when(mine)
+        def _():
+            some(31)
+
+        @pl.when(jnp.logical_not(mine))
+        def _():
+            some(32)
+
+    def project_half(low):
+        own = mm(by_pixel_v[...], from_tiles(hd_r[low : low + 32]).astype(BF))
+        rate = lax.rsqrt(jnp.mean(own * own, axis=-1, keepdims=True) + EPSILON)
+        normed = (own * rate * gain).astype(BF)
+        return [own, rate] + [mm(normed, w[...]).astype(BF) for w in (wq_v, wk_v, wv_v)]
+
+    wait_half(1, z < 4)
+    first = project_half(0)
+    wait_half(4, z >= 4)
+    second = project_half(32)
+    hidden, inverse, query, key, value = [
+        jnp.concatenate([a, b], 0) for a, b in zip(first, second)
+    ]
     token = iota((T, C), 0)
-    hidden = mm(by_pixel_v[...], from_tiles(hd_r[...]).astype(BF))
-    gain = gain_v[...]
-    inverse = lax.rsqrt(jnp.mean(hidden * hidden, axis=-1, keepdims=True) + EPSILON)
-    normed = (hidden * inverse * gain).astype(BF)
-    query = mm(normed, wq_v[...]).astype(BF)
-    key = mm(normed, wk_v[...]).astype(BF)
-    value = mm(normed, wv_v[...]).astype(BF)
     scale = 1.0 / 16.0
     causal = iota((128, 128), 1) <= iota((128, 128), 0)
-    parts = [slice(p * 128, p * 128 + 128) for p in range(4)]
-    scores = [mm_nt(query[r], key[r]) for r in parts]
-    prob_grad = [mm_nt(out_grad[r], value[r]) for r in parts]
+
+    def of(x, p):
+        return jnp.concatenate([x[p * 64 : p * 64 + 64], x[256 + p * 64 : 320 + p * 64]], 0)
+
+    def together(pixels):
+        return jnp.concatenate([x[:64] for x in pixels] + [x[64:] for x in pixels], 0)
+
+    queries, keys, values, grads = [
+        [of(x, p) for p in range(4)] for x in (query, key, value, out_grad)
+    ]
+    scores = [mm_nt(q, k) for q, k in zip(queries, keys)]
+    prob_grad = [mm_nt(g, v) for g, v in zip(grads, values)]
     weights = [jnp.where(causal, jnp.exp(x * scale), 0.0) for x in scores]
     probs = [w / jnp.sum(w, axis=-1, keepdims=True) for w in weights]
     centre = [jnp.sum(p * g, axis=-1, keepdims=True) for p, g in zip(probs, prob_grad)]
     score_grad = [
         (p * (g - c) * scale).astype(BF) for p, g, c in zip(probs, prob_grad, centre)
     ]
-    dv = [mm_tn(p.astype(BF), out_grad[r]).astype(BF) for p, r in zip(probs, parts)]
-    dq = [mm(g, key[r]).astype(BF) for g, r in zip(score_grad, parts)]
-    dk = [mm_tn(g, query[r]).astype(BF) for g, r in zip(score_grad, parts)]
+    dv = together([mm_tn(p.astype(BF), g).astype(BF) for p, g in zip(probs, grads)])
+    dq = together([mm(s, k).astype(BF) for s, k in zip(score_grad, keys)])
+    dk = together([mm_tn(s, q).astype(BF) for s, q in zip(score_grad, queries)])
     normed_grad = (
-        mm_nt(jnp.concatenate(dq, 0), wq_v[...])
-        + mm_nt(jnp.concatenate(dk, 0), wk_v[...])
-        + mm_nt(jnp.concatenate(dv, 0), wv_v[...])
+        mm_nt(dq, wq_v[...])
+        + mm_nt(dk, wk_v[...])
+        + mm_nt(dv, wv_v[...])
     )
     scaled = normed_grad * gain
     mean = jnp.mean(hidden * scaled, axis=-1, keepdims=True)
     attn_grad = (inverse * scaled - hidden * (inverse * inverse * inverse) * mean).astype(BF)
     total_p = (cot_p.astype(F32) + attn_grad.astype(F32)).astype(BF)
-    total_f = mm(by_frame_v[...], total_p)
+    total_f = jnp.concatenate(
+        [mm(by_frame_v[...], total_p[:256]), mm(by_frame_v[...], total_p[256:])], 0
+    )
     total_n = total_f.astype(BF)
     sgrad = (
         mm_nt(total_n, wt_v[0])
@@ -332,10 +367,12 @@
     for copy in ghalos:
         copy.wait()
     edges(ghalo_v, ws_v, pick_backward)
+    for f in range(2):
+        acc1[f] = columns(f, 0, 4)
     wait_all(tg_r, r_sem.at[3])
     total = mm(from_msg_v[...], from_tiles(tg_r[...]).astype(BF))
     for f in range(2):
-        out_v[f] = (total[f * 256 : f * 256 + 256] + columns(f, 0, 4)).astype(BF).reshape(4, 64, C)
+        out_v[f] = (total[f * 256 : f * 256 + 256] + acc1[f]).astype(BF).reshape(4, 64, C)
 
     @pl.when(me < 63)
     def _():
@@ -365,8 +402,8 @@
             vmem((2, 2, 64, C), BF), vmem((2, 2, 64, C), BF), vmem(big, BF), vmem(big, BF), vmem(big, BF),
             vmem((2, 256, C), F32), vmem((2, 256, C), F32), vmem((2, 256, C), F32),
             message, message, message, message, message, message, message, message,
-            vmem((T, T), BF), vmem((T, T), BF), vmem((T, T), BF), vmem((T, T), BF),
-            dma((9,)), dma((4,)), dma((4,)), dma((4,)), dma((4,)), dma((3,)), dma((3,)),
+            vmem((T, T), BF), vmem((T, T), BF), vmem((T // 2, T // 2), BF), vmem((T // 2, T // 2), BF),
+            dma((9,)), dma((4,)), dma((4,)), dma((4,)), dma((5,)), dma((3,)), dma((3,)),
             pltpu.SemaphoreType.REGULAR, pltpu.SemaphoreType.REGULAR((8,)),
         ],
         compiler_params=pltpu.CompilerParams(

time: 55 us -> 54.8 us (level)
  no operation moved by 1% of the time
where the time goes in v5:
time: 54.8 us; the launch traced here: 54.7 us
  Pallas kernels  54 us (99%)
  local copies, waits for them, and re-layouts  0.71 us (1%)
    pallas_call x1, Pallas kernels, body(): pl.pallas_call(kernel, out_shape=jax.ShapeDtypeStruct(big, BF), in_specs=...  54 us

profile of v5, /device:TPU:64, one launch (start us, length us, event | category | flops | bytes accessed | tf_op | source)
XLA Modules:
  0.0 54.7 jit_solution(6182749478531484680)
XLA Ops:
  0.0 54.0 %whole.1 = bf16[2,4,64,256]{3,2,1,0:T(8,128)(2,1)S(1)} custom-call(bf16[2,4,64,256]{3,2,1,0:T(8,128)(2,1)} %frames_h.1, bf16[2,4,64,256]{3,2,1,0:T(8,128)(2,1)} %cot_h.1, bf16[3,3,256,256]{3,2,1,0:T(8,128)(2,1)} %ws_h.1, bf16[3,256,256]{2,1,0:T(8,128)(2,1)} %wt_h.1, f32[1,256]{1,0:T(1,128)} %bitcast.1, bf16[256,256]{1,0:T(8,128)(2,1)} %wq_h.1, ...), custom_call_target="tpu_custom_call" | custom-call | tf_op jit(solution)/shard_map/whole/pallas_call | solution.py:394
  54.0 0.7 %copy.11 = bf16[2,4,64,256]{3,2,1,0:T(8,128)(2,1)} copy(bf16[2,4,64,256]{3,2,1,0:T(8,128)(2,1)S(1)} %whole.1) | data formatting | bytes 524288

commit v6 on v5

--- a/solution.py
+++ b/solution.py
@@ -30,7 +30,7 @@
 
 
 def to_tiles(x):
-    x = x.reshape(64, 8, C)
+    x = x.reshape(-1, 8, C)
     return jnp.concatenate([x[:, :, :128], x[:, :, 128:]], axis=1).astype(BF)
 
 
@@ -120,15 +120,19 @@
         send_row(src, dst, k, z, 7)
         dst[me] = src[me]
 
-    def send_ascending(src, dst, k):
-        def go(i, carry):
-            send_row(src, dst, k, i)
+    def send_rows(src, dst, k, low, high):
+        def go(row, carry):
+            @pl.when(row == z)
+            def _():
+                send_row(src, dst, k, z, 7)
+
+            @pl.when(row != z)
+            def _():
+                send_row(src, dst, k, row)
+
             return carry
 
-        lax.fori_loop(0, z, go, 0)
-        send_row(src, dst, k, z, 7)
-        lax.fori_loop(z + 1, 8, go, 0)
-        dst[me] = src[me]
+        lax.fori_loop(low, high, go, 0)
 
     def wait_all(dst, sem):
         pltpu.make_async_copy(dst.at[pl.ds(0, 63)], dst.at[pl.ds(0, 63)], sem).wait()
@@ -347,16 +351,26 @@
         [mm(by_frame_v[...], total_p[:256]), mm(by_frame_v[...], total_p[256:])], 0
     )
     total_n = total_f.astype(BF)
-    sgrad = (
-        mm_nt(total_n, wt_v[0])
-        + jnp.where(token >= T - 4, 0.0, roll_rows(mm_nt(total_n, wt_v[1]), -4))
-        + jnp.where(token >= T - 8, 0.0, roll_rows(mm_nt(total_n, wt_v[2]), -8))
+    ahead = total_n[:272]
+    sg_s[0:32] = to_tiles(
+        mm_nt(total_n[:256], wt_v[0])
+        + roll_rows(mm_nt(ahead, wt_v[1]), -4)[:256]
+        + mm_nt(ahead, wt_v[2])[8:264]
     )
-    sg_s[...] = to_tiles(sgrad)
-    send_ascending(sg_s, sg_r, 2)
+    send_rows(sg_s, sg_r, 2, 0, 4)
+    last = total_n[256:]
+    token = iota((T // 2, C), 0)
+    sg_s[32:64] = to_tiles(
+        mm_nt(last, wt_v[0])
+        + jnp.where(token >= 252, 0.0, roll_rows(mm_nt(last, wt_v[1]), -4))
+        + jnp.where(token >= 248, 0.0, roll_rows(mm_nt(last, wt_v[2]), -8))
+    )
+    send_rows(sg_s, sg_r, 2, 4, 8)
+    sg_r[me] = sg_s[me]
     tg_s[...] = to_tiles(total_f)
     wait_all(sg_s, s_sem.at[2])
-    send_ascending(tg_s, tg_r, 3)
+    send_rows(tg_s, tg_r, 3, 0, 8)
+    tg_r[me] = tg_s[me]
 
     wait_all(sg_r, r_sem.at[2])
     gnat_v[...] = mm(from_msg_v[...], from_tiles(sg_r[...]).astype(BF)).astype(BF).reshape(2, 4, 64, C)

time: 54.8 us -> 54.6 us (level)
  no operation moved by 1% of the time
where the time goes in v6:
time: 54.6 us; the launch traced here: 54.4 us
  Pallas kernels  53.7 us (98%)
  local copies, waits for them, and re-layouts  0.71 us (1%)
    pallas_call x1, Pallas kernels, body(): pl.pallas_call(kernel, out_shape=jax.ShapeDtypeStruct(big, BF), in_specs=...  53.7 us

profile of v6, /device:TPU:64, one launch (start us, length us, event | category | flops | bytes accessed | tf_op | source)
XLA Modules:
  0.0 54.4 jit_solution(12667055167808555162)
XLA Ops:
  0.0 53.7 %whole.1 = bf16[2,4,64,256]{3,2,1,0:T(8,128)(2,1)S(1)} custom-call(bf16[2,4,64,256]{3,2,1,0:T(8,128)(2,1)} %frames_h.1, bf16[2,4,64,256]{3,2,1,0:T(8,128)(2,1)} %cot_h.1, bf16[3,3,256,256]{3,2,1,0:T(8,128)(2,1)} %ws_h.1, bf16[3,256,256]{2,1,0:T(8,128)(2,1)} %wt_h.1, f32[1,256]{1,0:T(1,128)} %bitcast.1, bf16[256,256]{1,0:T(8,128)(2,1)} %wq_h.1, ...), custom_call_target="tpu_custom_call" | custom-call | tf_op jit(solution)/shard_map/whole/pallas_call | solution.py:408
  53.7 0.7 %copy.11 = bf16[2,4,64,256]{3,2,1,0:T(8,128)(2,1)} copy(bf16[2,4,64,256]{3,2,1,0:T(8,128)(2,1)S(1)} %whole.1) | data formatting | bytes 524288
